TPU v7x, 32 devices: a whole 2x2x4 slice. The times are simulated.
32 devices in a mesh: grp: 2 (over x), pool: 4 (over y, core), tp: 4 (over z).
Axes of the slice: x: 2, y: 2, z: 4, core: 2. Of those that a mesh axis runs over, the one named last changes fastest.
Arguments:
- queries: bfloat16 [3, 16, 6144], P(None, ('grp', 'pool'), 'tp'), parts along dimension 1, may hold values from -23 to 23
- new_kv: bfloat16 [3, 16, 2, 1024], P(None, ('grp', 'pool'), None, 'tp'), parts along dimension 1, may hold values from -5 to 5
- kv_cache: bfloat16 [3, 16, 2, 256, 1024], P(None, ('grp', 'pool'), None, None, 'tp'), parts along dimension 1, may hold values from -5 to 5
- cache_lengths: int32 [3, 16], P(None, ('grp', 'pool')), parts along dimension 1, may hold values from 1 to 256, 1024 in all within a row
- residual_in: bfloat16 [3, 16, 6144], P(None, 'grp', ('pool', 'tp')), parts along dimension 1, may hold values from -6 to 6
- out_weight: bfloat16 [6144, 6144], P('tp', 'pool'), may hold values from -0.625 to 0.625
- norm_gain: bfloat16 [6144], replicated, may hold values from 0.099609375 to 1.8984375
- router_weight: bfloat16 [6144, 4], replicated, may hold values from -0.078125 to 0.078125
- expert_in: bfloat16 [4, 2, 6144, 8192], P('pool', None, None, 'tp'), may hold values from -0.078125 to 0.078125
- expert_out: bfloat16 [4, 8192, 6144], P('pool', 'tp'), may hold values from -0.0625 to 0.0625
- expert_ids: int32 [3, 16, 2], P(None, 'grp'), parts along dimension 1, may hold values from 0 to 3, all different within a row; in each aligned block of 8 rows (0 to 7, 8 to 15, ..., all dimensions but the last counted through in order) at most 6 rows name the same one
Outputs:
- mixed_out: bfloat16 [3, 16, 6144], P(None, 'grp', ('pool', 'tp')), parts along dimension 1
There are 2 independent parts, one for each index of `grp`. A program takes and returns all parts, laid end to end along the dimension named above; an argument that names none is the same for every part. Nothing has to cross between parts.
Inputs may be any that keep to these rules, and one draw needn't show every extreme that they name: `expert_ids`: in each micro-batch no expert is named by more than 6 tokens, and the two ids of a token differ. `cache_lengths`: the lengths of one micro-batch sum to 1024.
All inputs are finite; a program needn't handle non-finite values. No bound on the sum of `cache_lengths` on one device may be relied on, other than what follows from the above.
Results may differ from a plain program's by a relative error of at most 0.014.
Values may be sent and summed in bfloat16 or wider, within the bound.
A program may use at most 192 MiB of HBM per device.

v0:
```python
import math

import jax
import jax.numpy as jnp
from jax import lax
from jax.sharding import PartitionSpec as P

HQ = 48
KVH = 8
HD = 128


def attend(query_rows, new_pairs, cache_rows, lengths):
    seq_count = query_rows.shape[0]
    kv_local = new_pairs.shape[-1] // HD
    group_q = HQ // KVH
    cache_len = cache_rows.shape[2]
    query_heads = query_rows.reshape(seq_count, kv_local, group_q, HD)
    key_rows = cache_rows[:, 0].reshape(seq_count, cache_len, kv_local, HD)
    value_rows = cache_rows[:, 1].reshape(seq_count, cache_len, kv_local, HD)
    new_keys = new_pairs[:, 0].reshape(seq_count, kv_local, HD)
    new_values = new_pairs[:, 1].reshape(seq_count, kv_local, HD)
    score_scale = 1.0 / math.sqrt(HD)
    old_scores = (
        jnp.einsum("sgqd,scgd->sgqc", query_heads, key_rows, preferred_element_type=jnp.float32)
        * score_scale
    )
    new_scores = (
        jnp.einsum("sgqd,sgd->sgq", query_heads, new_keys, preferred_element_type=jnp.float32)
        * score_scale
    )
    positions = jnp.arange(cache_len, dtype=jnp.int32)
    valid_mask = positions[None, :] < lengths[:, None]
    old_scores = jnp.where(valid_mask[:, None, None, :], old_scores, -jnp.inf)
    row_max = jnp.maximum(jnp.max(old_scores, axis=-1), new_scores)
    old_exp = jnp.exp(old_scores - row_max[..., None])
    new_exp = jnp.exp(new_scores - row_max)
    row_total = jnp.sum(old_exp, axis=-1) + new_exp
    old_probs = (old_exp / row_total[..., None]).astype(jnp.bfloat16)
    new_probs = (new_exp / row_total).astype(jnp.bfloat16)
    attended = jnp.einsum(
        "sgqc,scgd->sgqd", old_probs, value_rows, preferred_element_type=jnp.float32
    )
    attended = (
        attended
        + new_probs.astype(jnp.float32)[..., None] * new_values.astype(jnp.float32)[:, :, None, :]
    )
    return attended.reshape(seq_count, kv_local * group_q * HD).astype(jnp.bfloat16)


def shards(
    queries,
    new_kv,
    kv_cache,
    cache_lengths,
    residual_in,
    out_weight,
    norm_gain,
    router_weight,
    expert_in,
    expert_out,
    expert_ids,
):
    experts = router_weight.shape[1]
    pool_count = lax.axis_size("pool")
    tp_count = lax.axis_size("tp")
    group_size = pool_count // experts
    own_expert = lax.axis_index("pool") // group_size
    batches = queries.shape[0]
    token_count = residual_in.shape[1]
    col_width = residual_in.shape[2]
    capacity = 3 * token_count // 4
    slots_all = jnp.arange(experts * capacity, dtype=jnp.int32)
    expert_range = jnp.arange(experts, dtype=jnp.int32)
    self_hot = (expert_range == own_expert).astype(jnp.float32)
    gain_f = norm_gain.astype(jnp.float32)
    hiddens = []
    pick_tables = []
    own_tables = []
    buffer_rows = []
    other_slots = []
    for micro_batch in range(batches):
        attended = attend(
            queries[micro_batch],
            new_kv[micro_batch],
            kv_cache[micro_batch],
            cache_lengths[micro_batch],
        )
        heads_out = jnp.dot(
            lax.all_gather(attended, "pool", axis=0, tiled=True),
            out_weight,
            preferred_element_type=jnp.float32,
        )
        summed = lax.psum_scatter(
            heads_out.reshape(token_count, tp_count, col_width),
            "tp",
            scatter_dimension=1,
            tiled=True,
        )
        hidden = (
            residual_in[micro_batch].astype(jnp.float32) + summed.reshape(token_count, col_width)
        ).astype(jnp.bfloat16)
        hiddens.append(hidden)
        chosen_ids = expert_ids[micro_batch]
        id_hot = (chosen_ids[:, :, None] == expert_range[None, None, :]).astype(jnp.int32)
        chosen = jnp.sum(id_hot, axis=1)
        before = jnp.cumsum(chosen, axis=0) - chosen
        slot_index = jnp.sum(id_hot * before[:, None, :], axis=2)
        buffer_row = chosen_ids * capacity + slot_index
        buffer_rows.append(buffer_row)
        pick_table = jnp.any(buffer_row[None, :, :] == slots_all[:, None, None], axis=2).astype(
            jnp.bfloat16
        )
        pick_tables.append(pick_table)
        own_table = lax.dynamic_slice_in_dim(pick_table, own_expert * capacity, capacity, 0)
        own_tables.append(own_table)
        other_ids = jnp.where(chosen_ids[:, 0] == own_expert, chosen_ids[:, 1], chosen_ids[:, 0])
        other_hot = (other_ids[:, None] == expert_range[None, :]).astype(jnp.bfloat16)
        other_slots.append(jnp.dot(own_table, other_hot, preferred_element_type=jnp.float32))
    packed = jnp.concatenate(
        [
            jnp.dot(pick_tables[b], hiddens[b], preferred_element_type=jnp.bfloat16).reshape(
                experts, capacity, col_width
            )
            for b in range(batches)
        ],
        axis=1,
    )
    outgoing = jnp.repeat(packed, group_size * tp_count, axis=0)
    expert_rows = lax.all_to_all(outgoing, ("pool", "tp"), split_axis=0, concat_axis=2, tiled=True)[
        0
    ]
    rows_f = expert_rows.astype(jnp.float32)
    mean_sq = jnp.mean(rows_f * rows_f, axis=-1, keepdims=True)
    normed = (rows_f * lax.rsqrt(mean_sq + 1e-05) * gain_f).astype(jnp.bfloat16)
    logits = jnp.dot(normed, router_weight, preferred_element_type=jnp.float32)
    other_slot = jnp.concatenate(other_slots, axis=0)
    logit_self = jnp.sum(logits * self_hot[None, :], axis=1)
    logit_other = jnp.sum(logits * other_slot, axis=1)
    weight = jax.nn.sigmoid(logit_self - logit_other)
    gate_up = jnp.einsum("cd,kdf->kcf", normed, expert_in[0], preferred_element_type=jnp.float32)
    activated = (jax.nn.silu(gate_up[0]) * gate_up[1]).astype(jnp.bfloat16)
    partial_value = (
        jnp.dot(activated, expert_out[0], preferred_element_type=jnp.float32) * weight[:, None]
    )
    returned = lax.all_to_all(
        partial_value, ("pool", "tp"), split_axis=1, concat_axis=0, tiled=True
    )
    merged = jnp.sum(
        returned.reshape(experts, group_size * tp_count, batches, capacity, col_width), axis=1
    )
    results = []
    for micro_batch in range(batches):
        merged_batch = merged[:, micro_batch].reshape(experts * capacity, col_width)
        combined = jnp.sum(
            jnp.take(merged_batch, buffer_rows[micro_batch].reshape(-1), axis=0).reshape(
                token_count, 2, col_width
            ),
            axis=1,
        )
        results.append((hiddens[micro_batch].astype(jnp.float32) + combined).astype(jnp.bfloat16))
    return jnp.stack(results)


def solution(mesh):
    return jax.shard_map(
        shards,
        mesh=mesh,
        in_specs=(
            P(None, ("grp", "pool"), "tp"),
            P(None, ("grp", "pool"), None, "tp"),
            P(None, ("grp", "pool"), None, None, "tp"),
            P(None, ("grp", "pool")),
            P(None, "grp", ("pool", "tp")),
            P("tp", "pool"),
            P(),
            P(),
            P("pool", None, None, "tp"),
            P("pool", "tp", None),
            P(None, "grp", None),
        ),
        out_specs=P(None, "grp", ("pool", "tp")),
        check_vma=False,
    )
```

profile of v0, /device:TPU:0, one launch (start us, length us, event | category | flops | bytes accessed | tf_op | source)
XLA Modules:
  0.0 157.1 jit_solution(15729138633850079718)
XLA Ops:
  6.5 1.0 slice_reduce_fusion.2
  7.6 1.5 fusion.94
  9.0 0.2 copy.149
  9.5 0.2 fusion.101
  9.8 0.2 fusion.27
  10.0 0.2 fusion.14
  10.2 6.2 %all-gather.1 = bf16[4,2,1536]{2,1,0:T(2,128)(2,1)S(1)} all-gather(bf16[1,2,1536]{2,1,0:T(2,128)(2,1)S(1)} %reshape.331), channel_id=1, replica_groups=mesh['grp'=2,'pool'=4,'tp'=4] {'pool'}, dimensions={0}, use_global_device_ids=true | all-gather | bytes 30720 | tf_op jit(solution)/shard_map/all_gather | solution.py:90
  16.5 3.7 %fusion.104 = f32[8,1536]{1,0:T(8,128)} fusion(bf16[8,1536]{1,0:T(8,128)(2,1)S(1)} %reshape.332, bf16[1536,1536]{1,0:T(8,128)(2,1)} %param.18), kind=kOutput, calls=%fused_computation.197 | convolution fusion | flops 37748736 | bytes 4792320 | tf_op jit(solution)/shard_map/dot_general | solution.py:89
  20.2 0.2 copy.150
  20.6 0.2 fusion.100
  20.9 0.2 fusion.28
  21.1 0.2 fusion.15
  21.3 5.4 %all-gather.2 = bf16[4,2,1536]{2,1,0:T(2,128)(2,1)S(1)} all-gather(bf16[1,2,1536]{2,1,0:T(2,128)(2,1)S(1)} %reshape.333), channel_id=1, replica_groups=mesh['grp'=2,'pool'=4,'tp'=4] {'pool'}, dimensions={0}, use_global_device_ids=true | all-gather | bytes 30720 | tf_op jit(solution)/shard_map/all_gather | solution.py:90
  26.7 3.7 %fusion.105 = f32[8,1536]{1,0:T(8,128)} fusion(bf16[8,1536]{1,0:T(8,128)(2,1)S(1)} %reshape.334, bf16[1536,1536]{1,0:T(8,128)(2,1)} %param.18), kind=kOutput, calls=%fused_computation.198 | convolution fusion | flops 37748736 | bytes 4792320 | tf_op jit(solution)/shard_map/dot_general | solution.py:89
  30.5 0.2 copy.148
  30.9 0.2 fusion.102
  31.2 0.2 fusion.26
  31.4 0.2 fusion.13
  31.6 5.2 %all-gather = bf16[4,2,1536]{2,1,0:T(2,128)(2,1)S(1)} all-gather(bf16[1,2,1536]{2,1,0:T(2,128)(2,1)S(1)} %reshape.329), channel_id=1, replica_groups=mesh['grp'=2,'pool'=4,'tp'=4] {'pool'}, dimensions={0}, use_global_device_ids=true | all-gather | bytes 30720 | tf_op jit(solution)/shard_map/all_gather | solution.py:90
  36.8 3.7 %fusion.103 = f32[8,1536]{1,0:T(8,128)} fusion(bf16[8,1536]{1,0:T(8,128)(2,1)S(1)} %reshape.330, bf16[1536,1536]{1,0:T(8,128)(2,1)} %param.18), kind=kOutput, calls=%fused_computation.196 | convolution fusion | flops 37748736 | bytes 4792320 | tf_op jit(solution)/shard_map/dot_general | solution.py:89
  40.7 0.2 reduce_window_sum.24
  40.9 0.2 reduce_window_sum.25
  41.1 0.2 reduce_window_sum.20
  41.9 0.3 fusion.65
  42.1 0.3 fusion.66
  42.6 0.9 fusion.37
  43.5 17.0 %reduce-scatter.14.cloned.1.call-done = f32[8,1,384]{2,0,1:T(8,128)} async-done(((f32[8,4,384]{2,0,1:T(8,128)}), f32[8,1,384]{2,0,1:T(8,128)}) %reduce-scatter.14.cloned.1.call-update) | async-done | bytes 12304
  60.6 0.9 fusion.35
  61.5 18.6 %reduce-scatter.10.cloned.1.call-done = f32[8,1,384]{2,0,1:T(8,128)} async-done(((f32[8,4,384]{2,0,1:T(8,128)}), f32[8,1,384]{2,0,1:T(8,128)}) %reduce-scatter.10.cloned.1.call-update) | async-done | bytes 12304
  80.1 0.9 fusion.39
  81.0 0.7 broadcast_in_dim.36
  81.7 3.5 %all-to-all-start = ((bf16[16,18,384]{2,1,0:T(8,128)(2,1)}), bf16[16,18,384]{2,1,0:T(8,128)(2,1)S(1)}, u32[]{:S(2)}, u32[]{:S(2)}) async-start(bf16[16,18,384]{2,1,0:T(8,128)(2,1)} %bitcast.46), calls=%async_computation | async-start | bytes 589824 | tf_op jit(solution)/shard_map/all_to_all | solution.py:130
  85.3 0.3 fusion.67
  85.5 10.5 %all-to-all-done = bf16[16,18,384]{2,1,0:T(8,128)(2,1)S(1)} async-done(((bf16[16,18,384]{2,1,0:T(8,128)(2,1)}), bf16[16,18,384]{2,1,0:T(8,128)(2,1)S(1)}, u32[]{:S(2)}, u32[]{:S(2)}) %all-to-all-start) | async-done | bytes 221216 | tf_op jit(solution)/shard_map/all_to_all | solution.py:130
  96.0 0.2 fusion.16
  96.2 0.1 fusion.20
  96.4 0.1 reshape.353
  96.7 0.2 copy.151
  96.9 18.7 %fusion.7 = f32[2,18,2048]{2,1,0:T(8,128)S(1)} fusion(bf16[18,6144,1]{1,0,2:T(8,128)(2,1)S(1)} %reshape.353, bf16[1,2,6144,2048]{3,2,1,0:T(8,128)(2,1)} %param.21), kind=kOutput, calls=%fused_computation.8 | convolution fusion | flops 905969664 | bytes 50847744 | tf_op jit(solution)/shard_map/cd,kdf->kcf/dot_general | solution.py:141
  115.6 0.3 fusion.71
  115.9 9.9 %fusion.4 = f32[18,6144]{1,0:T(8,128)S(1)} fusion(bf16[1,2048,6144]{2,1,0:T(8,128)(2,1)} %param.22, f32[18]{0:T(128)S(1)} %add_divide_fusion, f32[2,18,2048]{2,1,0:T(8,128)S(1)} %fusion.7), kind=kOutput, calls=%fused_computation.7 | convolution fusion | flops 453316608 | bytes 25903176 | tf_op jit(solution)/shard_map/dot_general | solution.py:144
  126.0 1.0 copy.126
  127.0 3.6 %all-to-all-start.1 = ((f32[18,16,384]{2,0,1:T(8,128)}), f32[18,16,384]{2,0,1:T(8,128)S(1)}, u32[]{:S(2)}, u32[]{:S(2)}) async-start(f32[18,16,384]{2,0,1:T(8,128)} %copy.126), calls=%async_computation.1 | async-start | bytes 1179648 | tf_op jit(solution)/shard_map/all_to_all | solution.py:146
  131.3 16.3 %all-to-all-done.1 = f32[18,16,384]{2,0,1:T(8,128)S(1)} async-done(((f32[18,16,384]{2,0,1:T(8,128)}), f32[18,16,384]{2,0,1:T(8,128)S(1)}, u32[]{:S(2)}, u32[]{:S(2)}) %all-to-all-start.1) | async-done | bytes 442400 | tf_op jit(solution)/shard_map/all_to_all | solution.py:146
  147.7 0.6 gather_fusion.1
  148.5 0.6 gather_fusion.2
  149.2 0.6 gather_fusion
  150.0 0.6 pad_maximum_fusion.1
  (119 shorter events, 3.6 us)
Async XLA Ops:
  6.5 109.1 %copy-start = (bf16[6144,4]{0,1:T(4,128)(2,1)S(1)}, bf16[6144,4]{0,1:T(4,128)(2,1)}, u32[]{:S(2)}) copy-start(bf16[6144,4]{0,1:T(4,128)(2,1)} %param.20) | copy-start | bytes 147460
  6.5 2.7 %copy-start.6 = (bf16[3,2,1536]{2,1,0:T(2,128)(2,1)S(1)}, bf16[3,2,1536]{2,1,0:T(2,128)(2,1)}, u32[]{:S(2)}) copy-start(bf16[3,2,1536]{2,1,0:T(2,128)(2,1)} %param.13) | copy-start | bytes 55300
  6.5 2.8 %copy-start.8 = (bf16[3,2,2,256]{3,2,1,0:T(2,128)(2,1)S(1)}, bf16[3,2,2,256]{3,2,1,0:T(2,128)(2,1)}, u32[]{:S(2)}) copy-start(bf16[3,2,2,256]{3,2,1,0:T(2,128)(2,1)} %param.14) | copy-start | bytes 18436
  6.5 36.1 %reduce-scatter.12.cloned.1.call-start = ((), (), s32[]{:S(2)}) async-start(), calls=%async_computation.6 | async-start | bytes 61440
  20.2 40.4 %reduce-scatter.14.cloned.1.call-start = ((), (), s32[]{:S(2)}) async-start(), calls=%async_computation.7 | async-start | bytes 61440
  30.4 10.1 %copy-start.7 = (s32[3,8,2]{1,2,0:T(2,128)S(1)}, s32[3,8,2]{1,2,0:T(2,128)}, u32[]{:S(2)}) copy-start(s32[3,8,2]{1,2,0:T(2,128)} %param.23) | copy-start | bytes 580
  30.4 10.2 %copy-start.5 = (bf16[6144]{0:T(1024)(128)(2,1)S(1)}, bf16[6144]{0:T(1024)(128)(2,1)}, u32[]{:S(2)}) copy-start(bf16[6144]{0:T(1024)(128)(2,1)} %param.19) | copy-start | bytes 36868
  30.4 12.2 %copy-start.1 = (bf16[3,8,384]{2,1,0:T(8,128)(2,1)S(1)}, bf16[3,8,384]{2,1,0:T(8,128)(2,1)}, u32[]{:S(2)}) copy-start(bf16[3,8,384]{2,1,0:T(8,128)(2,1)} %param.17) | copy-start | bytes 55300
  30.4 49.6 %reduce-scatter.10.cloned.1.call-start = ((), (), s32[]{:S(2)}) async-start(), calls=%async_computation.5 | async-start | bytes 61440
  81.7 14.3 %all-to-all-start = ((bf16[16,18,384]{2,1,0:T(8,128)(2,1)}), bf16[16,18,384]{2,1,0:T(8,128)(2,1)S(1)}, u32[]{:S(2)}, u32[]{:S(2)}) async-start(bf16[16,18,384]{2,1,0:T(8,128)(2,1)} %bitcast.46), calls=%async_computation | async-start | bytes 589824 | tf_op jit(solution)/shard_map/all_to_all | solution.py:130
  125.8 24.1 %copy-start.2 = (f32[8,1,384]{2,0,1:T(8,128)S(1)}, f32[8,1,384]{2,0,1:T(8,128)}, u32[]{:S(2)}) copy-start(f32[8,1,384]{2,0,1:T(8,128)} %reduce-scatter.12.cloned.1.call-done) | copy-start | bytes 36868
  125.8 24.1 %copy-start.3 = (f32[8,1,384]{2,0,1:T(8,128)S(1)}, f32[8,1,384]{2,0,1:T(8,128)}, u32[]{:S(2)}) copy-start(f32[8,1,384]{2,0,1:T(8,128)} %reduce-scatter.14.cloned.1.call-done) | copy-start | bytes 36868
  125.9 24.1 %copy-start.4 = (f32[8,1,384]{2,0,1:T(8,128)S(1)}, f32[8,1,384]{2,0,1:T(8,128)}, u32[]{:S(2)}) copy-start(f32[8,1,384]{2,0,1:T(8,128)} %reduce-scatter.10.cloned.1.call-done) | copy-start | bytes 36868
  127.0 20.6 %all-to-all-start.1 = ((f32[18,16,384]{2,0,1:T(8,128)}), f32[18,16,384]{2,0,1:T(8,128)S(1)}, u32[]{:S(2)}, u32[]{:S(2)}) async-start(f32[18,16,384]{2,0,1:T(8,128)} %copy.126), calls=%async_computation.1 | async-start | bytes 1179648 | tf_op jit(solution)/shard_map/all_to_all | solution.py:146
Sparse Core Ops, SparseCore 0:
  20.3 20.6 reduce-scatter.11
  43.4 17.1 reduce-scatter.13
  62.8 17.2 reduce-scatter.9
where the time goes:
time: 158 us; the launch traced here: 157 us
  waiting for transfers between devices  62.5 us (40%)
  matrix products  45.1 us (29%)
  blocking collectives  16.8 us (11%)
  between operations  13.7 us (9%)
  local copies, waits for them, and re-layouts  8.81 us (6%)
  starting transfers between devices  7.2 us (5%)
  other arithmetic  3.1 us (2%)
    unnamed x6, waiting for transfers between devices  35.7 us
    dot_general x1, matrix products, shards(): jnp.einsum('cd,kdf->kcf', normed, expert_in[0], preferred_element_type=jn...  18.7 us
    all_gather x3, blocking collectives, shards(): lax.all_gather(attended, 'pool', axis=0, tiled=True)  16.8 us
    all_to_all x1, waiting for transfers between devices, shards(): lax.all_to_all(partial_value, ('pool', 'tp'), split_axis=1, concat_axis=0...  16.3 us
    dot_general x3, matrix products, shards(): jnp.dot(lax.all_gather(attended, 'pool', axis=0, tiled=True), out_weight,...  11 us
    all_to_all x1, waiting for transfers between devices, shards(): lax.all_to_all(outgoing, ('pool', 'tp'), split_axis=0, concat_axis=2, til...  10.5 us
    dot_general x1, matrix products, shards(): jnp.dot(activated, expert_out[0], preferred_element_type=jnp.float32)  9.92 us
    all_to_all x1, starting transfers between devices, shards(): lax.all_to_all(partial_value, ('pool', 'tp'), split_axis=1, concat_axis=0...  3.58 us
  transfers between devices with their start and end apart: 5, of which 4 were waited for; matrix products, arithmetic and copies ran while one was open for 9% of the time, Pallas kernels for 0%

commit v1 on v0

--- a/solution.py
+++ b/solution.py
@@ -1,8 +1,11 @@
+import functools
 import math
 
 import jax
 import jax.numpy as jnp
 from jax import lax
+from jax.experimental import pallas as pl
+from jax.experimental.pallas import tpu as pltpu
 from jax.sharding import PartitionSpec as P
 
 HQ = 48
@@ -162,9 +165,516 @@
     return jnp.stack(results)
 
 
+MESH = pl.DeviceIdType.MESH
+CHUNK = 256
+NT = (((1,), (1,)), ((), ()))
+
+
+def layer_kernel(
+    sizes,
+    lengths,
+    q_hbm,
+    nkv_hbm,
+    kv_hbm,
+    res_hbm,
+    wo_hbm,
+    gain_hbm,
+    router_hbm,
+    win_hbm,
+    wout_hbm,
+    ids_hbm,
+    out_ref,
+    q_v,
+    nkv_v,
+    kv_v,
+    res_v,
+    wo_v,
+    gain_v,
+    router_v,
+    ids_v,
+    slots,
+    qrow,
+    nkvf,
+    qh,
+    scores,
+    probs,
+    newp,
+    att,
+    att_all,
+    att_rows,
+    part_s,
+    part_r,
+    hid,
+    hid_all,
+    xn,
+    act,
+    mix_s,
+    mix_r,
+    mix_own,
+    fin,
+    fin_s,
+    fin_r,
+    small_sem,
+    kv_sem,
+    wo_sem,
+    in_sem,
+    out_sem,
+    att_ss,
+    att_rs,
+    part_ss,
+    part_rs,
+    hid_ss,
+    hid_rs,
+    mix_ss,
+    mix_rs,
+    fin_ss,
+    fin_rs,
+):
+    batches, seqs, kvl, group_q, hd, tokens, group_size = sizes
+    pool_n, tp_n = 4, 4
+    rows = batches * tokens
+    col = res_v.shape[2]
+    ffl = wout_hbm.shape[1]
+    chunks = win_hbm.shape[3] // CHUNK
+    half_w = mix_s.shape[3]
+    per_half = half_w // CHUNK
+    pool_w = tp_n * col
+
+    p = lax.axis_index("pool")
+    t = lax.axis_index("tp")
+    flip = 1 - 2 * (p % 2)
+    p_y = (p + 2) % 4
+    p_c = p + flip
+    p_yc = (p_y + flip) % 4
+    mates = (p_y, p_yc, p_c)
+    z_to = [(t + k) % tp_n for k in range(1, tp_n)]
+    z_from = [(t + tp_n - k) % tp_n for k in range(1, tp_n)]
+
+    barrier = pltpu.get_barrier_semaphore()
+    for mate in mates:
+        pl.semaphore_signal(barrier, inc=1, device_id={"pool": mate}, device_id_type=MESH)
+    for peer in z_to:
+        pl.semaphore_signal(barrier, inc=1, device_id={"tp": peer}, device_id_type=MESH)
+
+    smalls = [
+        pltpu.make_async_copy(src, dst, small_sem.at[i])
+        for i, (src, dst) in enumerate(
+            [
+                (q_hbm, q_v),
+                (nkv_hbm, nkv_v),
+                (res_hbm, res_v),
+                (gain_hbm, gain_v),
+                (router_hbm, router_v),
+                (ids_hbm, ids_v),
+            ]
+        )
+    ]
+    for copy in smalls[:2]:
+        copy.start()
+    kv_copy = pltpu.make_async_copy(kv_hbm, kv_v, kv_sem)
+    kv_copy.start()
+    for copy in smalls[2:]:
+        copy.start()
+    wo_copies = [
+        pltpu.make_async_copy(wo_hbm.at[:, pl.ds(k * col, col)], wo_v.at[k], wo_sem.at[k])
+        for k in range(tp_n)
+    ]
+    for copy in wo_copies:
+        copy.start()
+
+    def in_copy(j):
+        return pltpu.make_async_copy(
+            win_hbm.at[0, :, :, pl.ds(pl.multiple_of(j * CHUNK, CHUNK), CHUNK)],
+            slots.at[j],
+            in_sem.at[j],
+        )
+
+    def out_copy(slot, half, c, pool_block):
+        start = pool_block * pool_w + half * half_w + c * CHUNK
+        return pltpu.make_async_copy(
+            wout_hbm.at[0, :, pl.ds(pl.multiple_of(start, CHUNK), CHUNK)],
+            slots.at[slot, half, pl.ds(c * ffl, ffl), :],
+            out_sem.at[slot, half, c],
+        )
+
+    for copy in smalls[:2]:
+        copy.wait()
+    att[...] = jnp.zeros_like(att)
+    qh[...] = jnp.zeros_like(qh)
+    for b in range(batches):
+        qrow[pl.ds(b * seqs, seqs), :] = q_v[b].astype(jnp.float32)
+    for b in range(batches):
+        for s in range(seqs):
+            nkvf[b * seqs + s] = nkv_v[b, s].astype(jnp.float32)
+    for r in range(batches * seqs):
+        for g in range(kvl):
+            for h in range(group_q):
+                qh[pl.ds((r * kvl + g) * 8 + h, 1), :] = qrow[
+                    pl.ds(r, 1), pl.ds((g * group_q + h) * hd, hd)
+                ]
+    kv_copy.wait()
+
+    @pl.loop(0, chunks)
+    def _(j):
+        in_copy(j).start()
+
+    ctx = kv_v.shape[3]
+    scale = 1.0 / math.sqrt(hd)
+    place = lax.broadcasted_iota(jnp.int32, (8, ctx), 1)
+    news = []
+    for r in range(batches * seqs):
+        b, s = r // seqs, r % seqs
+        for g in range(kvl):
+            q8 = qh[pl.ds((r * kvl + g) * 8, 8), :]
+            keys = kv_v[b, s, 0, :, g * hd : (g + 1) * hd]
+            sc = (
+                lax.dot_general(
+                    q8.astype(jnp.bfloat16), keys, NT, preferred_element_type=jnp.float32
+                )
+                * scale
+            )
+            scores[pl.ds((r * kvl + g) * 8, 8), :] = jnp.where(
+                place < lengths[b, s], sc, -jnp.inf
+            )
+            nk = nkvf[r, 0:1, g * hd : (g + 1) * hd]
+            news.append(jnp.sum(q8 * nk, axis=1, keepdims=True) * scale)
+    new = jnp.concatenate(news, axis=0)
+    old = scores[...]
+    top = jnp.maximum(jnp.max(old, axis=1, keepdims=True), new)
+    old_exp = jnp.exp(old - top)
+    new_exp = jnp.exp(new - top)
+    total = jnp.sum(old_exp, axis=1, keepdims=True) + new_exp
+    probs[...] = old_exp / total
+    newp[...] = jnp.broadcast_to(
+        (new_exp / total).astype(jnp.bfloat16).astype(jnp.float32), newp.shape
+    )
+    for r in range(batches * seqs):
+        b, s = r // seqs, r % seqs
+        for g in range(kvl):
+            at = pl.ds((r * kvl + g) * 8, 8)
+            values = kv_v[b, s, 1, :, g * hd : (g + 1) * hd]
+            o8 = jnp.dot(
+                probs[at, :].astype(jnp.bfloat16), values, preferred_element_type=jnp.float32
+            )
+            o8 = o8 + newp[at, :] * nkvf[r, 1:2, g * hd : (g + 1) * hd]
+            for h in range(group_q):
+                att[r : r + 1, (g * group_q + h) * hd : (g * group_q + h + 1) * hd] = o8[h : h + 1]
+    att_all[p] = att[...].astype(jnp.bfloat16)
+
+    pl.semaphore_wait(barrier, len(mates) + len(z_to))
+
+    def send(src, dst, ss, rs, where):
+        return pltpu.make_async_remote_copy(
+            src_ref=src, dst_ref=dst, send_sem=ss, recv_sem=rs, device_id=where,
+            device_id_type=MESH,
+        )
+
+    sent = []
+    att_copies = []
+    for i, mate in enumerate(mates):
+        copy = send(att_all.at[p], att_all.at[p], att_ss.at[i], att_rs.at[i], {"pool": mate})
+        copy.start()
+        att_copies.append(copy)
+    for copy in wo_copies:
+        copy.wait()
+    for i, mate in enumerate(mates):
+        send(
+            att_all.at[mate], att_all.at[mate], att_ss.at[i], att_rs.at[i], {"pool": mate}
+        ).wait_recv()
+    sent += att_copies
+    for m in range(pool_n):
+        x = att_all[m].astype(jnp.float32)
+        for b in range(batches):
+            att_rows[pl.ds(b * tokens + m * seqs, seqs), :] = x[b * seqs : (b + 1) * seqs]
+    lhs = att_rows[...].astype(jnp.bfloat16)
+
+    for i, peer in enumerate(z_to):
+        part_s[i] = jnp.dot(lhs, wo_v[peer], preferred_element_type=jnp.float32).astype(
+            jnp.bfloat16
+        )
+        copy = send(part_s.at[i], part_r.at[i], part_ss.at[i], part_rs.at[i], {"tp": peer})
+        copy.start()
+        sent.append(copy)
+    summed = jnp.dot(lhs, wo_v[t], preferred_element_type=jnp.float32)
+    for copy in smalls[2:]:
+        copy.wait()
+    res = jnp.concatenate([res_v[b].astype(jnp.float32) for b in range(batches)], axis=0)
+    summed = summed + res
+    for i, peer in enumerate(z_to):
+        send(
+            part_s.at[i], part_r.at[i], part_ss.at[i], part_rs.at[i], {"tp": peer}
+        ).wait_recv()
+        summed = summed + part_r[i].astype(jnp.float32)
+    hidden = summed.astype(jnp.bfloat16)
+    hid[...] = hidden.astype(jnp.float32)
+    hid_all[p, t] = hidden
+
+    def hid_send(pp, tt, n, where):
+        return send(
+            hid_all.at[pp, tt], hid_all.at[pp, tt], hid_ss.at[n], hid_rs.at[pp, tt], where
+        )
+
+    for i, peer in enumerate(z_to):
+        copy = hid_send(p, t, i, {"tp": peer})
+        copy.start()
+        sent.append(copy)
+    order = [t] + z_from
+    n = tp_n - 1
+    for i, tt in enumerate(order):
+        if i > 0:
+            hid_send(p, tt, i - 1, {"tp": tt}).wait_recv()
+        for mate in (p_y, p_c):
+            copy = hid_send(p, tt, n, {"pool": mate})
+            copy.start()
+            sent.append(copy)
+            n += 1
+    for tt in order:
+        hid_send(p_y, tt, 0, {"pool": p_y}).wait_recv()
+        copy = hid_send(p_y, tt, n, {"pool": p_c})
+        copy.start()
+        sent.append(copy)
+        n += 1
+    for tt in order:
+        hid_send(p_c, tt, 0, {"pool": p_c}).wait_recv()
+    for tt in order:
+        hid_send(p_yc, tt, 0, {"pool": p_c}).wait_recv()
+
+    squares = jnp.zeros((rows, col), jnp.float32)
+    for m in range(pool_n):
+        for tt in range(tp_n):
+            h = hid_all[m, tt].astype(jnp.float32)
+            squares = squares + h * h
+    inv = lax.rsqrt(jnp.sum(squares, axis=1, keepdims=True) / (pool_n * pool_w) + 1e-05)
+    for m in range(pool_n):
+        for tt in range(tp_n):
+            h = hid_all[m, tt].astype(jnp.float32)
+            at = pl.ds((m * tp_n + tt) * col, col)
+            xn[:, at] = (h * inv * gain_v[:, at].astype(jnp.float32)).astype(jnp.bfloat16)
+    logits = lax.dot_general(xn[...], router_v[...], NT, preferred_element_type=jnp.float32)
+    experts = router_v.shape[0]
+    own = p // group_size
+    lane = lax.broadcasted_iota(jnp.int32, (tokens, experts), 1)
+    coeffs = []
+    for b in range(batches):
+        lb = logits[b * tokens : (b + 1) * tokens]
+        id0 = ids_v[b, :, 0:1]
+        id1 = ids_v[b, :, 1:2]
+        l0 = jnp.sum(jnp.where(lane == id0, lb, 0.0), axis=1, keepdims=True)
+        l1 = jnp.sum(jnp.where(lane == id1, lb, 0.0), axis=1, keepdims=True)
+        coeffs.append(
+            jnp.where(id0 == own, jax.nn.sigmoid(l0 - l1), 0.0)
+            + jnp.where(id1 == own, jax.nn.sigmoid(l1 - l0), 0.0)
+        )
+    coeff = jnp.concatenate(coeffs, axis=0)
+
+    def gate_up(j):
+        in_copy(j).wait()
+        gate = jnp.dot(xn[...], slots[j, 0], preferred_element_type=jnp.float32)
+        up = jnp.dot(xn[...], slots[j, 1], preferred_element_type=jnp.float32)
+        act[:, pl.ds(pl.multiple_of(j * CHUNK, CHUNK), CHUNK)] = (
+            jax.nn.silu(gate) * up
+        ).astype(jnp.bfloat16)
+
+    targets = mates + (p,)
+    for j in range(len(targets)):
+        gate_up(j)
+        for half in range(2):
+            for c in range(per_half):
+                out_copy(j, half, c, targets[j]).start()
+
+    @pl.loop(len(targets), chunks)
+    def _(j):
+        gate_up(j)
+
+    def down(slot, half, c):
+        out_copy(slot, half, c, targets[slot]).wait()
+        return (
+            jnp.dot(
+                act[...],
+                slots[slot, half, c * ffl : (c + 1) * ffl, :],
+                preferred_element_type=jnp.float32,
+            )
+            * coeff
+        )
+
+    for i, mate in enumerate(mates):
+        for half in range(2):
+            for c in range(per_half):
+                mix_s[i, half, :, c * CHUNK : (c + 1) * CHUNK] = down(i, half, c).astype(
+                    jnp.bfloat16
+                )
+            copy = send(
+                mix_s.at[i, half],
+                mix_r.at[i, half],
+                mix_ss.at[i, half],
+                mix_rs.at[i, half],
+                {"pool": mate},
+            )
+            copy.start()
+            sent.append(copy)
+    for half in range(2):
+        for c in range(per_half):
+            mix_own[half, :, c * CHUNK : (c + 1) * CHUNK] = down(len(mates), half, c)
+    for i, mate in enumerate(mates):
+        for half in range(2):
+            send(
+                mix_s.at[i, half],
+                mix_r.at[i, half],
+                mix_ss.at[i, half],
+                mix_rs.at[i, half],
+                {"pool": mate},
+            ).wait_recv()
+    for half in range(2):
+        whole = mix_own[half]
+        for i in range(len(mates)):
+            whole = whole + mix_r[i, half].astype(jnp.float32)
+        for k in range(2):
+            piece = whole[:, k * col : (k + 1) * col]
+            fin[half * 2 + k] = piece
+            fin_s[half * 2 + k] = piece.astype(jnp.bfloat16)
+    for i, peer in enumerate(z_to):
+        copy = send(fin_s.at[peer], fin_r.at[i], fin_ss.at[i], fin_rs.at[i], {"tp": peer})
+        copy.start()
+        sent.append(copy)
+    result = hid[...] + fin[t]
+    for i, peer in enumerate(z_to):
+        send(fin_s.at[peer], fin_r.at[i], fin_ss.at[i], fin_rs.at[i], {"tp": peer}).wait_recv()
+        result = result + fin_r[i].astype(jnp.float32)
+    for b in range(batches):
+        out_ref[b] = result[b * tokens : (b + 1) * tokens].astype(jnp.bfloat16)
+    for copy in sent:
+        copy.wait_send()
+
+
+def fused(
+    queries,
+    new_kv,
+    kv_cache,
+    cache_lengths,
+    residual_in,
+    out_weight,
+    norm_gain,
+    router_weight,
+    expert_in,
+    expert_out,
+    expert_ids,
+):
+    batches, seqs, q_width = queries.shape
+    tokens, col = residual_in.shape[1:]
+    rows = batches * tokens
+    kvl = new_kv.shape[3] // HD
+    group_q = HQ // KVH
+    model = norm_gain.shape[0]
+    experts = router_weight.shape[1]
+    ffl = expert_out.shape[1]
+    ctx = kv_cache.shape[3]
+    tp_n = 4
+    heads = batches * seqs * kvl * 8
+    half_w = tp_n * col // 2
+    per_half = half_w // CHUNK
+    chunks = ffl // CHUNK
+    bf, f32 = jnp.bfloat16, jnp.float32
+    dma = pltpu.SemaphoreType.DMA
+    sizes = (batches, seqs, kvl, group_q, HD, tokens, 4 // experts)
+    return pl.pallas_call(
+        functools.partial(layer_kernel, sizes),
+        out_shape=jax.ShapeDtypeStruct(residual_in.shape, bf),
+        in_specs=[pl.BlockSpec(memory_space=pltpu.SMEM)]
+        + [pl.BlockSpec(memory_space=pl.ANY)] * 10,
+        out_specs=pl.BlockSpec(memory_space=pltpu.VMEM),
+        scratch_shapes=[
+            pltpu.VMEM(queries.shape, bf),
+            pltpu.VMEM(new_kv.shape, bf),
+            pltpu.VMEM(kv_cache.shape, bf),
+            pltpu.VMEM(residual_in.shape, bf),
+            pltpu.VMEM((tp_n, q_width, col), bf),
+            pltpu.VMEM((1, model), bf),
+            pltpu.VMEM((experts, model), bf),
+            pltpu.VMEM(expert_ids.shape, jnp.int32),
+            pltpu.VMEM((chunks, 2, model, CHUNK), bf),
+            pltpu.VMEM((8, q_width), f32),
+            pltpu.VMEM((batches * seqs, 2, kvl * HD), f32),
+            pltpu.VMEM((heads, HD), f32),
+            pltpu.VMEM((heads, ctx), f32),
+            pltpu.VMEM((heads, ctx), f32),
+            pltpu.VMEM((heads, HD), f32),
+            pltpu.VMEM((8, q_width), f32),
+            pltpu.VMEM((4, 8, q_width), bf),
+            pltpu.VMEM((rows, q_width), f32),
+            pltpu.VMEM((tp_n - 1, rows, col), bf),
+            pltpu.VMEM((tp_n - 1, rows, col), bf),
+            pltpu.VMEM((rows, col), f32),
+            pltpu.VMEM((4, tp_n, rows, col), bf),
+            pltpu.VMEM((rows, model), bf),
+            pltpu.VMEM((rows, ffl), bf),
+            pltpu.VMEM((3, 2, rows, half_w), bf),
+            pltpu.VMEM((3, 2, rows, half_w), bf),
+            pltpu.VMEM((2, rows, half_w), f32),
+            pltpu.VMEM((tp_n, rows, col), f32),
+            pltpu.VMEM((tp_n, rows, col), bf),
+            pltpu.VMEM((tp_n - 1, rows, col), bf),
+            dma((6,)),
+            dma,
+            dma((tp_n,)),
+            dma((chunks,)),
+            dma((4, 2, per_half)),
+            dma((3,)),
+            dma((3,)),
+            dma((tp_n - 1,)),
+            dma((tp_n - 1,)),
+            dma((15,)),
+            dma((4, tp_n)),
+            dma((3, 2)),
+            dma((3, 2)),
+            dma((tp_n - 1,)),
+            dma((tp_n - 1,)),
+        ],
+        compiler_params=pltpu.CompilerParams(
+            collective_id=0, has_side_effects=True, vmem_limit_bytes=60 * 1024 * 1024
+        ),
+        cost_estimate=pl.CostEstimate(
+            flops=6 * rows * model * ffl,
+            bytes_accessed=6 * model * ffl + 2 * out_weight.size,
+            transcendentals=0,
+        ),
+        name="layer",
+    )(
+        cache_lengths,
+        queries,
+        new_kv,
+        kv_cache,
+        residual_in,
+        out_weight,
+        norm_gain.reshape(1, model),
+        router_weight.T,
+        expert_in,
+        expert_out,
+        expert_ids,
+    )
+
+
+def body(*arrays):
+    queries, new_kv, _, _, residual_in, _, norm_gain, router_weight, _, expert_out, _ = arrays
+    ffl, model = expert_out.shape[1:]
+    col = residual_in.shape[2]
+    fits = (
+        lax.axis_size("pool") == 4
+        and lax.axis_size("tp") == 4
+        and 4 % router_weight.shape[1] == 0
+        and col % 128 == 0
+        and (2 * col) % CHUNK == 0
+        and ffl % CHUNK == 0
+        and ffl // CHUNK >= 4
+        and 4 * col // CHUNK * ffl == 2 * model
+        and queries.shape[0] * queries.shape[1] <= 8
+        and residual_in.shape[1] % 8 == 0
+    )
+    return fused(*arrays) if fits else shards(*arrays)
+
+
 def solution(mesh):
     return jax.shard_map(
-        shards,
+        body,
         mesh=mesh,
         in_specs=(
             P(None, ("grp", "pool"), "tp"),

time: 158 us -> 51.7 us (0.33)
  waiting for transfers between devices: 62.5 us -> 0 us
  Pallas kernels: 0 us -> 46 us
  matrix products: 45.1 us -> 0 us
  blocking collectives: 16.8 us -> 0 us
  between operations: 13.7 us -> 0.01 us
  starting transfers between devices: 7.2 us -> 0 us
  local copies, waits for them, and re-layouts: 8.81 us -> 5.33 us
  other arithmetic: 3.1 us -> 0 us
    pallas_call x0 -> x1, Pallas kernels: none -> 46 us  [fused(): pl.pallas_call(functools.partial(layer_kernel, sizes), out_shape=jax.Shap...]
    dot_general x21 -> x0, matrix products: 45.1 us -> none  [the longest x1 18.7 us: shards(): jnp.einsum('cd,kdf->kcf', normed, expert_in[0], preferred_element_type=jn...]
    unnamed x6 -> x0, waiting for transfers between devices: 35.7 us -> none
    all_to_all x2 -> x0, waiting for transfers between devices: 26.8 us -> none  [the longest x1 16.3 us: shards(): lax.all_to_all(partial_value, ('pool', 'tp'), split_axis=1, concat_axis=0...]
    all_gather x3 -> x0, blocking collectives: 16.8 us -> none  [shards(): lax.all_gather(attended, 'pool', axis=0, tiled=True)]
    all_to_all x2 -> x0, starting transfers between devices: 7.12 us -> none  [the longest x1 3.58 us: shards(): lax.all_to_all(partial_value, ('pool', 'tp'), split_axis=1, concat_axis=0...]
    unnamed x31 -> x3, local copies, waits for them, and re-layouts: 1.13 us -> 4.02 us
    slice x10 -> x0, local copies, waits for them, and re-layouts: 2.63 us -> none  [the longest x1 1.47 us: shards(): kv_cache[micro_batch]]
  transfers between devices with their start and end apart: 5 -> 0, of which waited for: 4 -> 0; matrix products, arithmetic and copies ran while one was open for 9% -> 0% of each run, Pallas kernels for 0% -> 0%
where the time goes in v1:
time: 51.7 us; the launch traced here: 51.4 us
  Pallas kernels  46 us (89%)
  local copies, waits for them, and re-layouts  5.33 us (10%)
    pallas_call x1, Pallas kernels, fused(): pl.pallas_call(functools.partial(layer_kernel, sizes), out_shape=jax.Shap...  46 us
    unnamed x3, local copies, waits for them, and re-layouts  4.02 us
    reshape x1, local copies, waits for them, and re-layouts, fused(): norm_gain.reshape(1, model)  1.31 us

profile of v1, /device:TPU:0, one launch (start us, length us, event | category | flops | bytes accessed | tf_op | source)
XLA Modules:
  0.0 51.4 jit_solution(11767206055900832621)
XLA Ops:
  0.0 1.3 %copy.12.lengths = s32[3,2]{1,0:T(4,128)} copy(s32[3,2]{0,1:T(2,128)} %param.14) | data formatting | bytes 48 | tf_op args[3]
  1.3 1.4 %copy.13.ids_hbm = s32[3,8,2]{2,1,0:T(8,128)} copy(s32[3,8,2]{1,2,0:T(2,128)} %param.21) | data formatting | bytes 384 | tf_op args[10]
  2.7 1.3 %reshape.3.gain_hbm = bf16[1,6144]{1,0:T(2,128)(2,1)} reshape(bf16[6144]{0:T(1024)(128)(2,1)} %param.17) | data formatting | bytes 24576 | tf_op jit(solution)/shard_map/reshape | solution.py:648
  4.0 46.0 %layer.1 = bf16[3,8,384]{2,1,0:T(8,128)(2,1)} custom-call(s32[3,2]{1,0:T(4,128)} %copy.12.lengths, bf16[3,2,1536]{2,1,0:T(2,128)(2,1)} %q_hbm.1, bf16[3,2,2,256]{3,2,1,0:T(2,128)(2,1)} %nkv_hbm.1, bf16[3,2,2,256,256]{4,3,2,1,0:T(8,128)(2,1)} %kv_hbm.1, bf16[3,8,384]{2,1,0:T(8,128)(2,1)} %res_hbm.1, bf16[1536,1536]{1,0:T(8,128)(2,1)} %wo_hbm.1, ...), custom_call_target="tpu_custom_call" | custom-call | flops 1811939328 | bytes 80216064 | tf_op jit(solution)/shard_map/layer/pallas_call | solution.py:579
  50.1 1.3 %copy.15 = bf16[3,8,384]{2,1,0:T(8,128)(2,1)} copy(bf16[3,8,384]{2,1,0:T(8,128)(2,1)} %layer.1) | data formatting | bytes 36864

commit v2 on v1

--- a/solution.py
+++ b/solution.py
@@ -172,7 +172,7 @@
 
 def layer_kernel(
     sizes,
-    lengths,
+    len_hbm,
     q_hbm,
     nkv_hbm,
     kv_hbm,
@@ -184,36 +184,32 @@
     wout_hbm,
     ids_hbm,
     out_ref,
+    lengths,
     q_v,
     nkv_v,
     kv_v,
     res_v,
-    wo_v,
     gain_v,
     router_v,
     ids_v,
     slots,
-    qrow,
+    att,
     nkvf,
     qh,
     scores,
-    probs,
     newp,
-    att,
     att_all,
     att_rows,
     part_s,
     part_r,
     hid,
     hid_all,
+    gain_f,
     xn,
+    acc,
     act,
     mix_s,
     mix_r,
-    mix_own,
-    fin,
-    fin_s,
-    fin_r,
     small_sem,
     kv_sem,
     wo_sem,
@@ -227,8 +223,6 @@
     hid_rs,
     mix_ss,
     mix_rs,
-    fin_ss,
-    fin_rs,
 ):
     batches, seqs, kvl, group_q, hd, tokens, group_size = sizes
     pool_n, tp_n = 4, 4
@@ -236,7 +230,7 @@
     col = res_v.shape[2]
     ffl = wout_hbm.shape[1]
     chunks = win_hbm.shape[3] // CHUNK
-    half_w = mix_s.shape[3]
+    half_w = 2 * col
     per_half = half_w // CHUNK
     pool_w = tp_n * col
 
@@ -251,10 +245,12 @@
     z_from = [(t + tp_n - k) % tp_n for k in range(1, tp_n)]
 
     barrier = pltpu.get_barrier_semaphore()
-    for mate in mates:
-        pl.semaphore_signal(barrier, inc=1, device_id={"pool": mate}, device_id_type=MESH)
-    for peer in z_to:
-        pl.semaphore_signal(barrier, inc=1, device_id={"tp": peer}, device_id_type=MESH)
+    targets = mates + (p,)
+    others = [(m, z) for m in targets for z in z_to + [t]][:-1]
+    for mate, peer in others:
+        pl.semaphore_signal(
+            barrier, inc=1, device_id={"pool": mate, "tp": peer}, device_id_type=MESH
+        )
 
     smalls = [
         pltpu.make_async_copy(src, dst, small_sem.at[i])
@@ -262,6 +258,7 @@
             [
                 (q_hbm, q_v),
                 (nkv_hbm, nkv_v),
+                (len_hbm, lengths),
                 (res_hbm, res_v),
                 (gain_hbm, gain_v),
                 (router_hbm, router_v),
@@ -269,15 +266,21 @@
             ]
         )
     ]
-    for copy in smalls[:2]:
+    for copy in smalls[:3]:
         copy.start()
     kv_copy = pltpu.make_async_copy(kv_hbm, kv_v, kv_sem)
     kv_copy.start()
-    for copy in smalls[2:]:
+    for copy in smalls[3:]:
         copy.start()
+    q_width = wo_hbm.shape[0]
+    stack = slots.shape[2] // q_width
+
+    def wo_at(c):
+        return slots.at[chunks, c // stack, pl.ds(c % stack * q_width, q_width), :]
+
     wo_copies = [
-        pltpu.make_async_copy(wo_hbm.at[:, pl.ds(k * col, col)], wo_v.at[k], wo_sem.at[k])
-        for k in range(tp_n)
+        pltpu.make_async_copy(wo_hbm.at[:, pl.ds(c * CHUNK, CHUNK)], wo_at(c), wo_sem.at[c])
+        for c in range(pool_w // CHUNK)
     ]
     for copy in wo_copies:
         copy.start()
@@ -289,35 +292,43 @@
             in_sem.at[j],
         )
 
-    def out_copy(slot, half, c, pool_block):
-        start = pool_block * pool_w + half * half_w + c * CHUNK
+    far, near = 1 - t // 2, t // 2
+    groups = [(i, h) for h in (far, near) for i in range(pool_n)]
+    places = [chunks, 0, 1, 2]
+
+    def out_copy(n, c):
+        start = targets[groups[n][0]] * pool_w + groups[n][1] * half_w + c * CHUNK
         return pltpu.make_async_copy(
             wout_hbm.at[0, :, pl.ds(pl.multiple_of(start, CHUNK), CHUNK)],
-            slots.at[slot, half, pl.ds(c * ffl, ffl), :],
-            out_sem.at[slot, half, c],
-        )
-
-    for copy in smalls[:2]:
+            slots.at[places[n // 2], n % 2, pl.ds(c * ffl, ffl), :],
+            out_sem.at[n, c],
+        )
+
+    def start_pair(pair):
+        for n in (2 * pair, 2 * pair + 1):
+            for c in range(per_half):
+                out_copy(n, c).start()
+
+    for copy in smalls[:3]:
         copy.wait()
-    att[...] = jnp.zeros_like(att)
     qh[...] = jnp.zeros_like(qh)
     for b in range(batches):
-        qrow[pl.ds(b * seqs, seqs), :] = q_v[b].astype(jnp.float32)
+        att[pl.ds(b * seqs, seqs), :] = q_v[b].astype(jnp.float32)
     for b in range(batches):
         for s in range(seqs):
             nkvf[b * seqs + s] = nkv_v[b, s].astype(jnp.float32)
     for r in range(batches * seqs):
         for g in range(kvl):
             for h in range(group_q):
-                qh[pl.ds((r * kvl + g) * 8 + h, 1), :] = qrow[
+                qh[pl.ds((r * kvl + g) * 8 + h, 1), :] = att[
                     pl.ds(r, 1), pl.ds((g * group_q + h) * hd, hd)
                 ]
+    att[...] = jnp.zeros_like(att)
     kv_copy.wait()
 
     @pl.loop(0, chunks)
     def _(j):
         in_copy(j).start()
-
     ctx = kv_v.shape[3]
     scale = 1.0 / math.sqrt(hd)
     place = lax.broadcasted_iota(jnp.int32, (8, ctx), 1)
@@ -334,7 +345,7 @@
                 * scale
             )
             scores[pl.ds((r * kvl + g) * 8, 8), :] = jnp.where(
-                place < lengths[b, s], sc, -jnp.inf
+                place < lengths[s, b], sc, -jnp.inf
             )
             nk = nkvf[r, 0:1, g * hd : (g + 1) * hd]
             news.append(jnp.sum(q8 * nk, axis=1, keepdims=True) * scale)
@@ -344,7 +355,7 @@
     old_exp = jnp.exp(old - top)
     new_exp = jnp.exp(new - top)
     total = jnp.sum(old_exp, axis=1, keepdims=True) + new_exp
-    probs[...] = old_exp / total
+    scores[...] = old_exp / total
     newp[...] = jnp.broadcast_to(
         (new_exp / total).astype(jnp.bfloat16).astype(jnp.float32), newp.shape
     )
@@ -354,14 +365,14 @@
             at = pl.ds((r * kvl + g) * 8, 8)
             values = kv_v[b, s, 1, :, g * hd : (g + 1) * hd]
             o8 = jnp.dot(
-                probs[at, :].astype(jnp.bfloat16), values, preferred_element_type=jnp.float32
+                scores[at, :].astype(jnp.bfloat16), values, preferred_element_type=jnp.float32
             )
             o8 = o8 + newp[at, :] * nkvf[r, 1:2, g * hd : (g + 1) * hd]
             for h in range(group_q):
                 att[r : r + 1, (g * group_q + h) * hd : (g * group_q + h + 1) * hd] = o8[h : h + 1]
     att_all[p] = att[...].astype(jnp.bfloat16)
 
-    pl.semaphore_wait(barrier, len(mates) + len(z_to))
+    pl.semaphore_wait(barrier, len(others))
 
     def send(src, dst, ss, rs, where):
         return pltpu.make_async_remote_copy(
@@ -388,16 +399,27 @@
             att_rows[pl.ds(b * tokens + m * seqs, seqs), :] = x[b * seqs : (b + 1) * seqs]
     lhs = att_rows[...].astype(jnp.bfloat16)
 
+    for c in range(pool_w // CHUNK):
+        att_rows[:, c * CHUNK : (c + 1) * CHUNK] = jnp.dot(
+            lhs, wo_at(c)[...], preferred_element_type=jnp.float32
+        )
+
+    def piece_of(who):
+        return att_rows[:, pl.ds(pl.multiple_of(who * col, col), col)]
+
     for i, peer in enumerate(z_to):
-        part_s[i] = jnp.dot(lhs, wo_v[peer], preferred_element_type=jnp.float32).astype(
-            jnp.bfloat16
-        )
+        part_s[i] = piece_of(peer).astype(jnp.bfloat16)
         copy = send(part_s.at[i], part_r.at[i], part_ss.at[i], part_rs.at[i], {"tp": peer})
         copy.start()
         sent.append(copy)
-    summed = jnp.dot(lhs, wo_v[t], preferred_element_type=jnp.float32)
-    for copy in smalls[2:]:
+    start_pair(0)
+    summed = piece_of(t)
+    for copy in smalls[3:]:
         copy.wait()
+    for m in range(pool_n * tp_n):
+        gain_f[m : m + 1, :] = (
+            gain_v[m * col : (m + 1) * col].astype(jnp.float32).reshape(1, col)
+        )
     res = jnp.concatenate([res_v[b].astype(jnp.float32) for b in range(batches)], axis=0)
     summed = summed + res
     for i, peer in enumerate(z_to):
@@ -428,37 +450,58 @@
             copy.start()
             sent.append(copy)
             n += 1
+
+    def scaled(m):
+        total = jnp.zeros((rows, col), jnp.float32)
+        for tt in range(tp_n):
+            h = hid_all[m, tt].astype(jnp.float32)
+            total = total + h * h
+            xn[m, :, tt * col : (tt + 1) * col] = (h * gain_f[pl.ds(m * tp_n + tt, 1), :]).astype(jnp.bfloat16)
+        return total
+
+    def product(m, j, which):
+        k_rows = pl.ds(pl.multiple_of(m * pool_w, pool_w), pool_w)
+        return jnp.dot(xn[m], slots[j, which, k_rows, :], preferred_element_type=jnp.float32)
+
+    squares = scaled(p)
+
+    @pl.loop(0, chunks)
+    def _(j):
+        in_copy(j).wait()
+        for which in range(2):
+            acc[j, which] = product(p, j, which)
+
     for tt in order:
         hid_send(p_y, tt, 0, {"pool": p_y}).wait_recv()
         copy = hid_send(p_y, tt, n, {"pool": p_c})
         copy.start()
         sent.append(copy)
         n += 1
+    squares = squares + scaled(p_y)
     for tt in order:
         hid_send(p_c, tt, 0, {"pool": p_c}).wait_recv()
+    squares = squares + scaled(p_c)
     for tt in order:
         hid_send(p_yc, tt, 0, {"pool": p_c}).wait_recv()
-
-    squares = jnp.zeros((rows, col), jnp.float32)
-    for m in range(pool_n):
-        for tt in range(tp_n):
-            h = hid_all[m, tt].astype(jnp.float32)
-            squares = squares + h * h
+    squares = squares + scaled(p_yc)
     inv = lax.rsqrt(jnp.sum(squares, axis=1, keepdims=True) / (pool_n * pool_w) + 1e-05)
-    for m in range(pool_n):
-        for tt in range(tp_n):
-            h = hid_all[m, tt].astype(jnp.float32)
-            at = pl.ds((m * tp_n + tt) * col, col)
-            xn[:, at] = (h * inv * gain_v[:, at].astype(jnp.float32)).astype(jnp.bfloat16)
-    logits = lax.dot_general(xn[...], router_v[...], NT, preferred_element_type=jnp.float32)
+    logits = inv * sum(
+        lax.dot_general(
+            xn[m],
+            router_v[:, m * pool_w : (m + 1) * pool_w],
+            NT,
+            preferred_element_type=jnp.float32,
+        )
+        for m in range(pool_n)
+    )
     experts = router_v.shape[0]
     own = p // group_size
     lane = lax.broadcasted_iota(jnp.int32, (tokens, experts), 1)
     coeffs = []
     for b in range(batches):
         lb = logits[b * tokens : (b + 1) * tokens]
-        id0 = ids_v[b, :, 0:1]
-        id1 = ids_v[b, :, 1:2]
+        id0 = ids_v[b, 0:1, :].reshape(tokens, 1)
+        id1 = ids_v[b, 1:2, :].reshape(tokens, 1)
         l0 = jnp.sum(jnp.where(lane == id0, lb, 0.0), axis=1, keepdims=True)
         l1 = jnp.sum(jnp.where(lane == id1, lb, 0.0), axis=1, keepdims=True)
         coeffs.append(
@@ -468,78 +511,69 @@
     coeff = jnp.concatenate(coeffs, axis=0)
 
     def gate_up(j):
-        in_copy(j).wait()
-        gate = jnp.dot(xn[...], slots[j, 0], preferred_element_type=jnp.float32)
-        up = jnp.dot(xn[...], slots[j, 1], preferred_element_type=jnp.float32)
+        gate, up = [
+            inv * (acc[j, which] + sum(product(m, j, which) for m in mates)) for which in range(2)
+        ]
         act[:, pl.ds(pl.multiple_of(j * CHUNK, CHUNK), CHUNK)] = (
             jax.nn.silu(gate) * up
         ).astype(jnp.bfloat16)
 
-    targets = mates + (p,)
-    for j in range(len(targets)):
+    for j in range(3):
         gate_up(j)
-        for half in range(2):
-            for c in range(per_half):
-                out_copy(j, half, c, targets[j]).start()
-
-    @pl.loop(len(targets), chunks)
+        start_pair(j + 1)
+
+    @pl.loop(3, chunks)
     def _(j):
         gate_up(j)
 
-    def down(slot, half, c):
-        out_copy(slot, half, c, targets[slot]).wait()
-        return (
-            jnp.dot(
-                act[...],
-                slots[slot, half, c * ffl : (c + 1) * ffl, :],
-                preferred_element_type=jnp.float32,
+    def mix_send(n, e, i, peer):
+        k = (peer + tp_n - t) % tp_n
+        return send(
+            mix_s.at[n, e],
+            mix_r.at[i, k],
+            mix_ss.at[n, e],
+            mix_rs.at[i, k],
+            {"pool": targets[i], "tp": peer},
+        )
+
+    for n, (i, h) in enumerate(groups):
+        parts = []
+        for c in range(per_half):
+            out_copy(n, c).wait()
+            parts.append(
+                jnp.dot(
+                    act[...],
+                    slots[places[n // 2], n % 2, c * ffl : (c + 1) * ffl, :],
+                    preferred_element_type=jnp.float32,
+                )
             )
-            * coeff
-        )
-
-    for i, mate in enumerate(mates):
-        for half in range(2):
-            for c in range(per_half):
-                mix_s[i, half, :, c * CHUNK : (c + 1) * CHUNK] = down(i, half, c).astype(
-                    jnp.bfloat16
-                )
-            copy = send(
-                mix_s.at[i, half],
-                mix_r.at[i, half],
-                mix_ss.at[i, half],
-                mix_rs.at[i, half],
-                {"pool": mate},
-            )
-            copy.start()
-            sent.append(copy)
-    for half in range(2):
-        for c in range(per_half):
-            mix_own[half, :, c * CHUNK : (c + 1) * CHUNK] = down(len(mates), half, c)
-    for i, mate in enumerate(mates):
-        for half in range(2):
-            send(
-                mix_s.at[i, half],
-                mix_r.at[i, half],
-                mix_ss.at[i, half],
-                mix_rs.at[i, half],
-                {"pool": mate},
-            ).wait_recv()
-    for half in range(2):
-        whole = mix_own[half]
-        for i in range(len(mates)):
-            whole = whole + mix_r[i, half].astype(jnp.float32)
-        for k in range(2):
-            piece = whole[:, k * col : (k + 1) * col]
-            fin[half * 2 + k] = piece
-            fin_s[half * 2 + k] = piece.astype(jnp.bfloat16)
-    for i, peer in enumerate(z_to):
-        copy = send(fin_s.at[peer], fin_r.at[i], fin_ss.at[i], fin_rs.at[i], {"tp": peer})
-        copy.start()
-        sent.append(copy)
-    result = hid[...] + fin[t]
-    for i, peer in enumerate(z_to):
-        send(fin_s.at[peer], fin_r.at[i], fin_ss.at[i], fin_rs.at[i], {"tp": peer}).wait_recv()
-        result = result + fin_r[i].astype(jnp.float32)
+        whole = jnp.concatenate(parts, axis=1) * coeff
+        for e in range(2):
+            piece = whole[:, e * col : (e + 1) * col]
+            mix_s[n, e] = piece.astype(jnp.bfloat16)
+            if n < len(groups) - 1:
+                copy = mix_send(n, e, i, 2 * h + e)
+                copy.start()
+                sent.append(copy)
+            else:
+                att_rows[:, e * col : (e + 1) * col] = piece
+    last = len(groups) - 1
+    copy = mix_send(last, 1 - t % 2, pool_n - 1, t + 1 - 2 * (t % 2))
+    copy.start()
+    sent.append(copy)
+    result = hid[...] + piece_of(t % 2)
+    for k in range(tp_n):
+        for i in range(pool_n):
+            if i < pool_n - 1 or k > 0:
+                pltpu.make_async_remote_copy(
+                    src_ref=mix_r.at[i, k],
+                    dst_ref=mix_r.at[i, k],
+                    send_sem=mix_ss.at[0, 0],
+                    recv_sem=mix_rs.at[i, k],
+                    device_id={"pool": targets[i], "tp": (t + tp_n - k) % tp_n},
+                    device_id_type=MESH,
+                ).wait_recv()
+                result = result + mix_r[i, k].astype(jnp.float32)
     for b in range(batches):
         out_ref[b] = result[b * tokens : (b + 1) * tokens].astype(jnp.bfloat16)
     for copy in sent:
@@ -579,58 +613,51 @@
     return pl.pallas_call(
         functools.partial(layer_kernel, sizes),
         out_shape=jax.ShapeDtypeStruct(residual_in.shape, bf),
-        in_specs=[pl.BlockSpec(memory_space=pltpu.SMEM)]
-        + [pl.BlockSpec(memory_space=pl.ANY)] * 10,
+        in_specs=[pl.BlockSpec(memory_space=pl.ANY)] * 11,
         out_specs=pl.BlockSpec(memory_space=pltpu.VMEM),
         scratch_shapes=[
+            pltpu.SMEM((seqs, batches), jnp.int32),
             pltpu.VMEM(queries.shape, bf),
             pltpu.VMEM(new_kv.shape, bf),
             pltpu.VMEM(kv_cache.shape, bf),
             pltpu.VMEM(residual_in.shape, bf),
-            pltpu.VMEM((tp_n, q_width, col), bf),
-            pltpu.VMEM((1, model), bf),
+            pltpu.VMEM((model,), bf),
             pltpu.VMEM((experts, model), bf),
-            pltpu.VMEM(expert_ids.shape, jnp.int32),
-            pltpu.VMEM((chunks, 2, model, CHUNK), bf),
+            pltpu.VMEM((batches, 2, tokens), jnp.int32),
+            pltpu.VMEM((chunks + 1, 2, model, CHUNK), bf),
             pltpu.VMEM((8, q_width), f32),
             pltpu.VMEM((batches * seqs, 2, kvl * HD), f32),
             pltpu.VMEM((heads, HD), f32),
             pltpu.VMEM((heads, ctx), f32),
-            pltpu.VMEM((heads, ctx), f32),
             pltpu.VMEM((heads, HD), f32),
-            pltpu.VMEM((8, q_width), f32),
             pltpu.VMEM((4, 8, q_width), bf),
             pltpu.VMEM((rows, q_width), f32),
             pltpu.VMEM((tp_n - 1, rows, col), bf),
             pltpu.VMEM((tp_n - 1, rows, col), bf),
             pltpu.VMEM((rows, col), f32),
             pltpu.VMEM((4, tp_n, rows, col), bf),
-            pltpu.VMEM((rows, model), bf),
+            pltpu.VMEM((4 * tp_n, col), f32),
+            pltpu.VMEM((4, rows, tp_n * col), bf),
+            pltpu.VMEM((chunks, 2, rows, CHUNK), f32),
             pltpu.VMEM((rows, ffl), bf),
-            pltpu.VMEM((3, 2, rows, half_w), bf),
-            pltpu.VMEM((3, 2, rows, half_w), bf),
-            pltpu.VMEM((2, rows, half_w), f32),
-            pltpu.VMEM((tp_n, rows, col), f32),
-            pltpu.VMEM((tp_n, rows, col), bf),
-            pltpu.VMEM((tp_n - 1, rows, col), bf),
-            dma((6,)),
+            pltpu.VMEM((8, 2, rows, col), bf),
+            pltpu.VMEM((4, tp_n, rows, col), bf),
+            dma((7,)),
             dma,
-            dma((tp_n,)),
+            dma((tp_n * col // CHUNK,)),
             dma((chunks,)),
-            dma((4, 2, per_half)),
+            dma((8, per_half)),
             dma((3,)),
             dma((3,)),
             dma((tp_n - 1,)),
             dma((tp_n - 1,)),
             dma((15,)),
             dma((4, tp_n)),
-            dma((3, 2)),
-            dma((3, 2)),
-            dma((tp_n - 1,)),
-            dma((tp_n - 1,)),
+            dma((8, 2)),
+            dma((4, tp_n)),
         ],
         compiler_params=pltpu.CompilerParams(
-            collective_id=0, has_side_effects=True, vmem_limit_bytes=60 * 1024 * 1024
+            collective_id=0, has_side_effects=True, vmem_limit_bytes=63 * 1024 * 1024
         ),
         cost_estimate=pl.CostEstimate(
             flops=6 * rows * model * ffl,
@@ -639,17 +666,17 @@
         ),
         name="layer",
     )(
-        cache_lengths,
+        cache_lengths.T,
         queries,
         new_kv,
         kv_cache,
         residual_in,
         out_weight,
-        norm_gain.reshape(1, model),
+        norm_gain,
         router_weight.T,
         expert_in,
         expert_out,
-        expert_ids,
+        expert_ids.transpose(0, 2, 1),
     )
 
 
@@ -666,6 +693,8 @@
         and ffl % CHUNK == 0
         and ffl // CHUNK >= 4
         and 4 * col // CHUNK * ffl == 2 * model
+        and 4 * col // CHUNK * queries.shape[2] <= 2 * model
+        and queries.shape[2] == 4 * col
         and queries.shape[0] * queries.shape[1] <= 8
         and residual_in.shape[1] % 8 == 0
     )

time: 51.7 us -> 43.6 us (0.84)
  local copies, waits for them, and re-layouts: 5.33 us -> 1.33 us
  Pallas kernels: 46 us -> 42.1 us
    pallas_call x1, Pallas kernels: 46 us -> 42.1 us  [fused(): pl.pallas_call(functools.partial(layer_kernel, sizes), out_shape=jax.Shap...]
    unnamed x3 -> x1, local copies, waits for them, and re-layouts: 4.02 us -> 1.33 us
    reshape x1 -> x0, local copies, waits for them, and re-layouts: 1.31 us -> none  [fused(): norm_gain.reshape(1, model)]
where the time goes in v2:
time: 43.6 us; the launch traced here: 43.4 us
  Pallas kernels  42.1 us (97%)
  local copies, waits for them, and re-layouts  1.33 us (3%)
    pallas_call x1, Pallas kernels, fused(): pl.pallas_call(functools.partial(layer_kernel, sizes), out_shape=jax.Shap...  42.1 us
    unnamed x1, local copies, waits for them, and re-layouts  1.33 us

profile of v2, /device:TPU:0, one launch (start us, length us, event | category | flops | bytes accessed | tf_op | source)
XLA Modules:
  0.0 43.4 jit_solution(6661868882348735256)
XLA Ops:
  0.0 42.1 %layer.1 = bf16[3,8,384]{2,1,0:T(8,128)(2,1)} custom-call(s32[2,3]{1,0:T(2,128)} %bitcast.5, bf16[3,2,1536]{2,1,0:T(2,128)(2,1)} %q_hbm.1, bf16[3,2,2,256]{3,2,1,0:T(2,128)(2,1)} %nkv_hbm.1, bf16[3,2,2,256,256]{4,3,2,1,0:T(8,128)(2,1)} %kv_hbm.1, bf16[3,8,384]{2,1,0:T(8,128)(2,1)} %res_hbm.1, bf16[1536,1536]{1,0:T(8,128)(2,1)} %wo_hbm.1, ...), custom_call_target="tpu_custom_call" | custom-call | flops 1811939328 | bytes 80216064 | tf_op jit(solution)/shard_map/layer/pallas_call | solution.py:613
  42.1 1.3 %copy.13 = bf16[3,8,384]{2,1,0:T(8,128)(2,1)} copy(bf16[3,8,384]{2,1,0:T(8,128)(2,1)} %layer.1) | data formatting | bytes 36864

commit v3 on v2

--- a/solution.py
+++ b/solution.py
@@ -273,23 +273,26 @@
     for copy in smalls[3:]:
         copy.start()
     q_width = wo_hbm.shape[0]
-    stack = slots.shape[2] // q_width
+    wide = 2 * CHUNK
 
     def wo_at(c):
-        return slots.at[chunks, c // stack, pl.ds(c % stack * q_width, q_width), :]
+        return slots.at[chunks, pl.ds(c * q_width, q_width), :]
 
     wo_copies = [
-        pltpu.make_async_copy(wo_hbm.at[:, pl.ds(c * CHUNK, CHUNK)], wo_at(c), wo_sem.at[c])
-        for c in range(pool_w // CHUNK)
+        pltpu.make_async_copy(wo_hbm.at[:, pl.ds(c * wide, wide)], wo_at(c), wo_sem.at[c])
+        for c in range(pool_w // wide)
     ]
     for copy in wo_copies:
         copy.start()
 
-    def in_copy(j):
+    def in_copy(j, i, which):
+        from_row = pl.multiple_of(targets[i] * pool_w, pool_w)
         return pltpu.make_async_copy(
-            win_hbm.at[0, :, :, pl.ds(pl.multiple_of(j * CHUNK, CHUNK), CHUNK)],
-            slots.at[j],
-            in_sem.at[j],
+            win_hbm.at[
+                0, which, pl.ds(from_row, pool_w), pl.ds(pl.multiple_of(j * CHUNK, CHUNK), CHUNK)
+            ],
+            slots.at[j, pl.ds(i * pool_w, pool_w), pl.ds(which * CHUNK, CHUNK)],
+            in_sem.at[j, i, which],
         )
 
     far, near = 1 - t // 2, t // 2
@@ -300,7 +303,11 @@
         start = targets[groups[n][0]] * pool_w + groups[n][1] * half_w + c * CHUNK
         return pltpu.make_async_copy(
             wout_hbm.at[0, :, pl.ds(pl.multiple_of(start, CHUNK), CHUNK)],
-            slots.at[places[n // 2], n % 2, pl.ds(c * ffl, ffl), :],
+            slots.at[
+                places[n // 2],
+                pl.ds((n % 2 * per_half + c) // 2 * ffl, ffl),
+                pl.ds((n % 2 * per_half + c) % 2 * CHUNK, CHUNK),
+            ],
             out_sem.at[n, c],
         )
 
@@ -328,7 +335,9 @@
 
     @pl.loop(0, chunks)
     def _(j):
-        in_copy(j).start()
+        for i in range(pool_n):
+            for which in range(2):
+                in_copy(j, i, which).start()
     ctx = kv_v.shape[3]
     scale = 1.0 / math.sqrt(hd)
     place = lax.broadcasted_iota(jnp.int32, (8, ctx), 1)
@@ -399,8 +408,8 @@
             att_rows[pl.ds(b * tokens + m * seqs, seqs), :] = x[b * seqs : (b + 1) * seqs]
     lhs = att_rows[...].astype(jnp.bfloat16)
 
-    for c in range(pool_w // CHUNK):
-        att_rows[:, c * CHUNK : (c + 1) * CHUNK] = jnp.dot(
+    for c in range(pool_w // wide):
+        att_rows[:, c * wide : (c + 1) * wide] = jnp.dot(
             lhs, wo_at(c)[...], preferred_element_type=jnp.float32
         )
 
@@ -451,25 +460,25 @@
             sent.append(copy)
             n += 1
 
-    def scaled(m):
+    def scaled(i):
+        m = targets[i]
         total = jnp.zeros((rows, col), jnp.float32)
         for tt in range(tp_n):
             h = hid_all[m, tt].astype(jnp.float32)
             total = total + h * h
-            xn[m, :, tt * col : (tt + 1) * col] = (h * gain_f[pl.ds(m * tp_n + tt, 1), :]).astype(jnp.bfloat16)
+            xn[:, i * pool_w + tt * col : i * pool_w + (tt + 1) * col] = (
+                h * gain_f[pl.ds(m * tp_n + tt, 1), :]
+            ).astype(jnp.bfloat16)
         return total
 
-    def product(m, j, which):
-        k_rows = pl.ds(pl.multiple_of(m * pool_w, pool_w), pool_w)
-        return jnp.dot(xn[m], slots[j, which, k_rows, :], preferred_element_type=jnp.float32)
-
-    squares = scaled(p)
+    squares = scaled(pool_n - 1)
+    cut = (pool_n - 1) * pool_w
 
     @pl.loop(0, chunks)
     def _(j):
-        in_copy(j).wait()
         for which in range(2):
-            acc[j, which] = product(p, j, which)
+            in_copy(j, pool_n - 1, which).wait()
+        acc[j] = jnp.dot(xn[:, cut:], slots[j, cut:, :], preferred_element_type=jnp.float32)
 
     for tt in order:
         hid_send(p_y, tt, 0, {"pool": p_y}).wait_recv()
@@ -477,22 +486,22 @@
         copy.start()
         sent.append(copy)
         n += 1
-    squares = squares + scaled(p_y)
+    squares = squares + scaled(0)
     for tt in order:
         hid_send(p_c, tt, 0, {"pool": p_c}).wait_recv()
-    squares = squares + scaled(p_c)
+    squares = squares + scaled(2)
     for tt in order:
         hid_send(p_yc, tt, 0, {"pool": p_c}).wait_recv()
-    squares = squares + scaled(p_yc)
+    squares = squares + scaled(1)
     inv = lax.rsqrt(jnp.sum(squares, axis=1, keepdims=True) / (pool_n * pool_w) + 1e-05)
     logits = inv * sum(
         lax.dot_general(
-            xn[m],
-            router_v[:, m * pool_w : (m + 1) * pool_w],
+            xn[:, i * pool_w : (i + 1) * pool_w],
+            router_v[:, pl.ds(pl.multiple_of(m * pool_w, pool_w), pool_w)],
             NT,
             preferred_element_type=jnp.float32,
         )
-        for m in range(pool_n)
+        for i, m in enumerate(targets)
     )
     experts = router_v.shape[0]
     own = p // group_size
@@ -511,9 +520,14 @@
     coeff = jnp.concatenate(coeffs, axis=0)
 
     def gate_up(j):
-        gate, up = [
-            inv * (acc[j, which] + sum(product(m, j, which) for m in mates)) for which in range(2)
-        ]
+        for i in range(pool_n - 1):
+            for which in range(2):
+                in_copy(j, i, which).wait()
+        both = inv * (
+            acc[j]
+            + jnp.dot(xn[:, :cut], slots[j, :cut, :], preferred_element_type=jnp.float32)
+        )
+        gate, up = both[:, :CHUNK], both[:, CHUNK:]
         act[:, pl.ds(pl.multiple_of(j * CHUNK, CHUNK), CHUNK)] = (
             jax.nn.silu(gate) * up
         ).astype(jnp.bfloat16)
@@ -536,18 +550,24 @@
             {"pool": targets[i], "tp": peer},
         )
 
+    def down(pair, c):
+        return jnp.dot(
+            act[...],
+            slots[places[pair], c * ffl : (c + 1) * ffl, :],
+            preferred_element_type=jnp.float32,
+        )
+
     for n, (i, h) in enumerate(groups):
-        parts = []
-        for c in range(per_half):
+        for c in range(n % 2, per_half):
             out_copy(n, c).wait()
-            parts.append(
-                jnp.dot(
-                    act[...],
-                    slots[places[n // 2], n % 2, c * ffl : (c + 1) * ffl, :],
-                    preferred_element_type=jnp.float32,
-                )
+        if n % 2 == 0:
+            out_copy(n + 1, 0).wait()
+            out_cols = [down(n // 2, 0), down(n // 2, 1)]
+            whole = jnp.concatenate([out_cols[0], out_cols[1][:, :CHUNK]], axis=1) * coeff
+        else:
+            whole = (
+                jnp.concatenate([out_cols[1][:, CHUNK:], down(n // 2, 2)], axis=1) * coeff
             )
-        whole = jnp.concatenate(parts, axis=1) * coeff
         for e in range(2):
             piece = whole[:, e * col : (e + 1) * col]
             mix_s[n, e] = piece.astype(jnp.bfloat16)
@@ -624,7 +644,7 @@
             pltpu.VMEM((model,), bf),
             pltpu.VMEM((experts, model), bf),
             pltpu.VMEM((batches, 2, tokens), jnp.int32),
-            pltpu.VMEM((chunks + 1, 2, model, CHUNK), bf),
+            pltpu.VMEM((chunks + 1, model, 2 * CHUNK), bf),
             pltpu.VMEM((8, q_width), f32),
             pltpu.VMEM((batches * seqs, 2, kvl * HD), f32),
             pltpu.VMEM((heads, HD), f32),
@@ -637,15 +657,15 @@
             pltpu.VMEM((rows, col), f32),
             pltpu.VMEM((4, tp_n, rows, col), bf),
             pltpu.VMEM((4 * tp_n, col), f32),
-            pltpu.VMEM((4, rows, tp_n * col), bf),
-            pltpu.VMEM((chunks, 2, rows, CHUNK), f32),
+            pltpu.VMEM((rows, model), bf),
+            pltpu.VMEM((chunks, rows, 2 * CHUNK), f32),
             pltpu.VMEM((rows, ffl), bf),
             pltpu.VMEM((8, 2, rows, col), bf),
             pltpu.VMEM((4, tp_n, rows, col), bf),
             dma((7,)),
             dma,
-            dma((tp_n * col // CHUNK,)),
-            dma((chunks,)),
+            dma((tp_n * col // (2 * CHUNK),)),
+            dma((chunks, 4, 2)),
             dma((8, per_half)),
             dma((3,)),
             dma((3,)),
@@ -689,11 +709,10 @@
         and lax.axis_size("tp") == 4
         and 4 % router_weight.shape[1] == 0
         and col % 128 == 0
-        and (2 * col) % CHUNK == 0
+        and 2 * col == 3 * CHUNK
         and ffl % CHUNK == 0
         and ffl // CHUNK >= 4
         and 4 * col // CHUNK * ffl == 2 * model
-        and 4 * col // CHUNK * queries.shape[2] <= 2 * model
         and queries.shape[2] == 4 * col
         and queries.shape[0] * queries.shape[1] <= 8
         and residual_in.shape[1] % 8 == 0

time: 43.6 us -> 44 us (level)
  no operation moved by 1% of the time
where the time goes in v3:
time: 44 us; the launch traced here: 43.8 us
  Pallas kernels  42.5 us (97%)
  local copies, waits for them, and re-layouts  1.33 us (3%)
    pallas_call x1, Pallas kernels, fused(): pl.pallas_call(functools.partial(layer_kernel, sizes), out_shape=jax.Shap...  42.5 us
    unnamed x1, local copies, waits for them, and re-layouts  1.33 us

profile of v3, /device:TPU:0, one launch (start us, length us, event | category | flops | bytes accessed | tf_op | source)
XLA Modules:
  0.0 43.8 jit_solution(6486101164653032345)
XLA Ops:
  0.0 42.5 %layer.1 = bf16[3,8,384]{2,1,0:T(8,128)(2,1)} custom-call(s32[2,3]{1,0:T(2,128)} %bitcast.5, bf16[3,2,1536]{2,1,0:T(2,128)(2,1)} %q_hbm.1, bf16[3,2,2,256]{3,2,1,0:T(2,128)(2,1)} %nkv_hbm.1, bf16[3,2,2,256,256]{4,3,2,1,0:T(8,128)(2,1)} %kv_hbm.1, bf16[3,8,384]{2,1,0:T(8,128)(2,1)} %res_hbm.1, bf16[1536,1536]{1,0:T(8,128)(2,1)} %wo_hbm.1, ...), custom_call_target="tpu_custom_call" | custom-call | flops 1811939328 | bytes 80216064 | tf_op jit(solution)/shard_map/layer/pallas_call | solution.py:633
  42.5 1.3 %copy.13 = bf16[3,8,384]{2,1,0:T(8,128)(2,1)} copy(bf16[3,8,384]{2,1,0:T(8,128)(2,1)} %layer.1) | data formatting | bytes 36864

commit v4 on v2

--- a/solution.py
+++ b/solution.py
@@ -440,6 +440,20 @@
         copy = hid_send(p, t, i, {"tp": peer})
         copy.start()
         sent.append(copy)
+
+    def scaled(m):
+        total = jnp.zeros((rows, col), jnp.float32)
+        for tt in range(tp_n):
+            h = hid_all[m, tt].astype(jnp.float32)
+            total = total + h * h
+            xn[m, :, tt * col : (tt + 1) * col] = (h * gain_f[pl.ds(m * tp_n + tt, 1), :]).astype(jnp.bfloat16)
+        return total
+
+    def product(m, j, which):
+        k_rows = pl.ds(pl.multiple_of(m * pool_w, pool_w), pool_w)
+        return jnp.dot(xn[m], slots[j, which, k_rows, :], preferred_element_type=jnp.float32)
+
+    squares = jnp.zeros((rows, col), jnp.float32)
     order = [t] + z_from
     n = tp_n - 1
     for i, tt in enumerate(order):
@@ -450,26 +464,19 @@
             copy.start()
             sent.append(copy)
             n += 1
-
-    def scaled(m):
-        total = jnp.zeros((rows, col), jnp.float32)
-        for tt in range(tp_n):
-            h = hid_all[m, tt].astype(jnp.float32)
-            total = total + h * h
-            xn[m, :, tt * col : (tt + 1) * col] = (h * gain_f[pl.ds(m * tp_n + tt, 1), :]).astype(jnp.bfloat16)
-        return total
-
-    def product(m, j, which):
-        k_rows = pl.ds(pl.multiple_of(m * pool_w, pool_w), pool_w)
-        return jnp.dot(xn[m], slots[j, which, k_rows, :], preferred_element_type=jnp.float32)
-
-    squares = scaled(p)
-
-    @pl.loop(0, chunks)
-    def _(j):
-        in_copy(j).wait()
-        for which in range(2):
-            acc[j, which] = product(p, j, which)
+        h = hid_all[p, tt].astype(jnp.float32)
+        squares = squares + h * h
+        x = (h * gain_f[pl.ds(p * tp_n + tt, 1), :]).astype(jnp.bfloat16)
+        xn[p, :, pl.ds(pl.multiple_of(tt * col, col), col)] = x
+        k_rows = pl.ds(pl.multiple_of((p * tp_n + tt) * col, col), col)
+
+        @pl.loop(0, chunks)
+        def _(j, i=i, x=x, k_rows=k_rows):
+            if i == 0:
+                in_copy(j).wait()
+            for which in range(2):
+                term = jnp.dot(x, slots[j, which, k_rows, :], preferred_element_type=jnp.float32)
+                acc[j, which] = term if i == 0 else acc[j, which] + term
 
     for tt in order:
         hid_send(p_y, tt, 0, {"pool": p_y}).wait_recv()

time: 43.6 us -> 48.9 us (1.12)
  Pallas kernels: 42.1 us -> 47.4 us
    pallas_call x1, Pallas kernels: 42.1 us -> 47.4 us  [fused(): pl.pallas_call(functools.partial(layer_kernel, sizes), out_shape=jax.Shap...]
where the time goes in v4:
time: 48.9 us; the launch traced here: 48.7 us
  Pallas kernels  47.4 us (97%)
  local copies, waits for them, and re-layouts  1.33 us (3%)
    pallas_call x1, Pallas kernels, fused(): pl.pallas_call(functools.partial(layer_kernel, sizes), out_shape=jax.Shap...  47.4 us
    unnamed x1, local copies, waits for them, and re-layouts  1.33 us

profile of v4, /device:TPU:0, one launch (start us, length us, event | category | flops | bytes accessed | tf_op | source)
XLA Modules:
  0.0 48.7 jit_solution(18175442912781916281)
XLA Ops:
  0.0 47.4 %layer.1 = bf16[3,8,384]{2,1,0:T(8,128)(2,1)} custom-call(s32[2,3]{1,0:T(2,128)} %bitcast.5, bf16[3,2,1536]{2,1,0:T(2,128)(2,1)} %q_hbm.1, bf16[3,2,2,256]{3,2,1,0:T(2,128)(2,1)} %nkv_hbm.1, bf16[3,2,2,256,256]{4,3,2,1,0:T(8,128)(2,1)} %kv_hbm.1, bf16[3,8,384]{2,1,0:T(8,128)(2,1)} %res_hbm.1, bf16[1536,1536]{1,0:T(8,128)(2,1)} %wo_hbm.1, ...), custom_call_target="tpu_custom_call" | custom-call | flops 1811939328 | bytes 80216064 | tf_op jit(solution)/shard_map/layer/pallas_call | solution.py:620
  47.4 1.3 %copy.13 = bf16[3,8,384]{2,1,0:T(8,128)(2,1)} copy(bf16[3,8,384]{2,1,0:T(8,128)(2,1)} %layer.1) | data formatting | bytes 36864
